TPU v7x, 32 devices: a whole 2x2x4 slice. The times are simulated.
32 devices in a mesh: dp: 16 (over z, y, x), seq: 2 (over core).
Axes of the slice: x: 2, y: 2, z: 4, core: 2. Of those that a mesh axis runs over, the one named last changes fastest.
Arguments:
- labels: int32 [32], P('dp'), may hold values from 0 to 1000
- targets: int32 [32, 256], P('dp', 'seq'), may hold values from 0 to 16383
- heights: int32 [32], P('dp'), may hold values from 8 to 16, as said below
- loss_mask: int32 [32, 256], P('dp', 'seq'), may hold values from 0 to 1
- class_table: float32 [1001, 768], P(None, ('dp', 'seq')), may hold values from -1.8 to 1.8
- code_table: float32 [16384, 768], P(('dp', 'seq')), may hold values from -1.8 to 1.8
- attend_in: float32 [768, 2304], P(('dp', 'seq')), may hold values from -0.21875 to 0.21875
- attend_mix: float32 [768, 768], P(('dp', 'seq')), may hold values from -0.625 to 0.625
- expand_in: float32 [768, 4096], P(('dp', 'seq')), may hold values from -0.21875 to 0.21875
- shrink_out: float32 [2048, 768], P(('dp', 'seq')), may hold values from -0.125 to 0.125
- head_weight: float32 [768, 16384], P(None, ('dp', 'seq')), may hold values from -0.21875 to 0.21875
- norm_gains: float32 [3, 768], P(None, ('dp', 'seq')), may hold values from 0.34 to 2.3
- drift_class: float32 [1001, 768], P(None, ('dp', 'seq')), may hold values from -1.1920929e-07 to 1.1920929e-07
- drift_code: float32 [16384, 768], P(('dp', 'seq')), may hold values from -2.9802322e-07 to 2.9802322e-07
- drift_attend: float32 [768, 2304], P(('dp', 'seq')), may hold values from -2.861023e-06 to 2.861023e-06
- drift_mix: float32 [768, 768], P(('dp', 'seq')), may hold values from -2.861023e-06 to 2.861023e-06
- drift_expand: float32 [768, 4096], P(('dp', 'seq')), may hold values from -2.861023e-06 to 2.861023e-06
- drift_shrink: float32 [2048, 768], P(('dp', 'seq')), may hold values from -2.861023e-06 to 2.861023e-06
- drift_head: float32 [768, 16384], P(None, ('dp', 'seq')), may hold values from -2.861023e-06 to 2.861023e-06
- drift_gains: float32 [3, 768], P(None, ('dp', 'seq')), may hold values from -1.1444092e-05 to 1.1444092e-05
- square_class: float32 [1001, 768], P(None, ('dp', 'seq')), may hold values from 1.4031683e-16 to 1.1204005e-15
- square_code: float32 [16384, 768], P(('dp', 'seq')), may hold values from 7.942518e-16 to 6.3419343e-15
- square_attend: float32 [768, 2304], P(('dp', 'seq')), may hold values from 7.966128e-14 to 1.2721573e-12
- square_mix: float32 [768, 768], P(('dp', 'seq')), may hold values from 7.966128e-14 to 1.2721573e-12
- square_expand: float32 [768, 4096], P(('dp', 'seq')), may hold values from 7.966128e-14 to 1.2721573e-12
- square_shrink: float32 [2048, 768], P(('dp', 'seq')), may hold values from 7.966128e-14 to 1.2721573e-12
- square_head: float32 [768, 16384], P(None, ('dp', 'seq')), may hold values from 7.966128e-14 to 1.2721573e-12
- square_gains: float32 [3, 768], P(None, ('dp', 'seq')), may hold values from 1.2721573e-12 to 2.0293938e-11
Outputs:
- class_new: float32 [1001, 768], P(None, ('dp', 'seq'))
- code_new: float32 [16384, 768], P(('dp', 'seq'))
- attend_new: float32 [768, 2304], P(('dp', 'seq'))
- mix_new: float32 [768, 768], P(('dp', 'seq'))
- expand_new: float32 [768, 4096], P(('dp', 'seq'))
- shrink_new: float32 [2048, 768], P(('dp', 'seq'))
- head_new: float32 [768, 16384], P(None, ('dp', 'seq'))
- gains_new: float32 [3, 768], P(None, ('dp', 'seq'))
- momentum_class: float32 [1001, 768], P(None, ('dp', 'seq'))
- momentum_code: float32 [16384, 768], P(('dp', 'seq'))
- momentum_attend: float32 [768, 2304], P(('dp', 'seq'))
- momentum_mix: float32 [768, 768], P(('dp', 'seq'))
- momentum_expand: float32 [768, 4096], P(('dp', 'seq'))
- momentum_shrink: float32 [2048, 768], P(('dp', 'seq'))
- momentum_head: float32 [768, 16384], P(None, ('dp', 'seq'))
- momentum_gains: float32 [3, 768], P(None, ('dp', 'seq'))
- variance_class: float32 [1001, 768], P(None, ('dp', 'seq'))
- variance_code: float32 [16384, 768], P(('dp', 'seq'))
- variance_attend: float32 [768, 2304], P(('dp', 'seq'))
- variance_mix: float32 [768, 768], P(('dp', 'seq'))
- variance_expand: float32 [768, 4096], P(('dp', 'seq'))
- variance_shrink: float32 [2048, 768], P(('dp', 'seq'))
- variance_head: float32 [768, 16384], P(None, ('dp', 'seq'))
- variance_gains: float32 [3, 768], P(None, ('dp', 'seq'))
- grad_norm: float32 [], replicated
- loss_sum: float32 [], replicated
- loss_count: float32 [], replicated
Inputs may be any that keep to these rules, and one draw needn't show every extreme that they name: `heights`: in each aligned block of 2 images (those of one index of dp) at least one image has 16 rows.
All inputs are finite; a program needn't handle non-finite values.
Results may differ from a plain program's by a relative error of at most 0.02.
The roundings to bfloat16 on the way count: a program that leaves them out, or rounds other values in their place, can miss the bound.
Values may be sent and summed in bfloat16 or wider, within the bound.
A program may use at most 320 MiB of HBM per device.

v0:
```python
import functools

import jax
import jax.numpy as jnp
import numpy as np
from jax import lax
from jax.experimental import pallas as pl
from jax.experimental.pallas import tpu as pltpu
from jax.sharding import PartitionSpec as P

HD = 64
GRID = 16
STEP = 10

EPS_NORM = 1e-05
BETA_ONE = 0.9
BETA_TWO = 0.95
ADAM_EPS = 1e-08
CLIP_NORM = 0.01
NEGATIVE_FILL = -1000000000.0
RATES = (0.8, 0.8, 0.08, 0.08, 0.08, 0.08, 0.08, 0.8)
DECAYS = (0.1, 0.1, 0.1, 0.1, 0.1, 0.1, 0.1, 0.0)

PIECE = 512

MESH = pl.DeviceIdType.MESH
ANY = pl.BlockSpec(memory_space=pl.ANY)
VMEM = pl.BlockSpec(memory_space=pltpu.VMEM)
SMEM = pl.BlockSpec(memory_space=pltpu.SMEM)
BF = jnp.bfloat16
F32 = jnp.float32


def dims_of(dp):
    bits = dp.bit_length() - 1
    nz = 1 << (bits // 2)
    rest = dp // nz
    ny = 1 << ((rest.bit_length() - 1) // 2)
    return (nz, ny, rest // ny)


class Place:
    def __init__(self, dims):
        self.dims = dims
        nz, ny, nx = dims
        chip = lax.axis_index("dp")
        self.c = lax.axis_index("seq")
        self.z = chip // (ny * nx)
        self.y = (chip // nx) % ny
        self.x = chip % nx

    def zs(self, back):
        return (self.z + self.dims[0] - back) % self.dims[0]

    def ys(self, back):
        return (self.y + self.dims[1] - back) % self.dims[1]

    def xs(self, back):
        return (self.x + self.dims[2] - back) % self.dims[2]

    def dev(self, z=0, y=0, x=0, c=0):
        nz, ny, nx = self.dims
        z, y, x = ((self.z + z) % nz, (self.y + y) % ny, (self.x + x) % nx)
        return ((z * ny + y) * nx + x, (self.c + c) % 2)


def line_offsets(dims):
    nz, ny, nx = dims
    return (
        [(s, 0, 0, 0) for s in range(1, nz)]
        + [(0, s, 0, 0) for s in range(1, ny)]
        + [(0, 0, s, 0) for s in range(1, nx)]
        + [(0, 0, 0, 1)]
    )


def plane_offsets(dims):
    return [(0, v, u, 0) for v in range(dims[1]) for u in range(dims[2]) if v or u]


def greet(place, offsets):
    offsets = sorted(set(offsets))
    sem = pltpu.get_barrier_semaphore()
    for off in offsets:
        pl.semaphore_signal(sem, inc=1, device_id=place.dev(*off), device_id_type=MESH)
    pl.semaphore_wait(sem, len(offsets))


class Comm:
    def __init__(self, send_sems, recv_sems, local_sems):
        self.send_sems, self.recv_sems, self.local_sems = (send_sems, recv_sems, local_sems)
        self.sent, self.held, self.count, self.locals = ([], [], 0, 0)

    def send(self, src, dst, device):
        k = self.count
        self.count += 1
        copy = pltpu.make_async_remote_copy(
            src_ref=src,
            dst_ref=dst,
            send_sem=self.send_sems.at[k],
            recv_sem=self.recv_sems.at[k],
            device_id=device,
            device_id_type=MESH,
        )
        copy.start()
        self.sent.append(copy)
        return copy

    def keep(self, src, dst):
        copy = pltpu.make_async_copy(src, dst, self.local_sems.at[self.locals])
        self.locals += 1
        copy.start()
        self.held.append(copy)
        return copy

    def gone(self, copy):
        copy.wait_send()
        self.sent = [other for other in self.sent if other is not copy]

    def done(self, copy):
        copy.wait()
        self.held = [other for other in self.held if other is not copy]

    def finish(self):
        for copy in self.sent:
            copy.wait_send()
        for copy in self.held:
            copy.wait()


def drain(steps):
    for _ in steps:
        pass


def all_offsets(dims):
    nz, ny, nx = dims
    spots = [(k, j, i, core) for k in range(nz) for j in range(ny) for i in range(nx) for core in range(2)]
    return spots[1:]


def small_exchange(comm, place, src, out, own):
    z, y, x, c = (place.z, place.y, place.x, place.c)
    nz, ny, nx = place.dims
    if own:
        comm.keep(src(z, y, x, c), out.at[z, y, x, c])
    got = []
    for off in all_offsets(place.dims):
        there = (place.zs(nz - off[0]), place.ys(ny - off[1]), place.xs(nx - off[2]), (c + off[3]) % 2)
        got.append(comm.send(src(*there), out.at[z, y, x, c], place.dev(*off)))
    return got


class PlaneGather:
    def __init__(self, comm, place):
        self.comm, self.place = (comm, place)
        self.firsts, self.seconds, self.mates = ([], [], [])

    def ways(self, axis):
        _, ny, nx = self.place.dims
        return range(1, ny if axis == "y" else nx)

    def back(self, axis, t, yy, xx):
        return (self.place.ys(t), xx) if axis == "y" else (yy, self.place.xs(t))

    def spread(self, block, first, src=None):
        place, second = (self.place, "y" if first == "x" else "x")
        dst = block(place.y, place.x)
        src = dst if src is None else src
        for t in self.ways(first):
            copy = self.comm.send(src, dst, place.dev(**{first: t}))
            self.firsts.append((block, first, second, t, copy))
        for t in self.ways(second):
            copy = self.comm.send(src, dst, place.dev(**{second: t}))
            self.seconds.append((block(*self.back(second, t, place.y, place.x)), copy))
        self.mates.append(self.comm.send(src, dst, place.dev(c=1)))

    def forward(self):
        place = self.place
        for block, first, second, t, copy in self.firsts:
            copy.wait_recv()
            yy, xx = self.back(first, t, place.y, place.x)
            held = block(yy, xx)
            for u in self.ways(second):
                copy = self.comm.send(held, held, place.dev(**{second: u}))
                self.seconds.append((block(*self.back(second, u, yy, xx)), copy))
            self.mates.append(self.comm.send(held, held, place.dev(c=1)))
        self.firsts = []

    def settle(self):
        for held, copy in self.seconds:
            copy.wait_recv()
            self.mates.append(self.comm.send(held, held, self.place.dev(c=1)))
        self.seconds = []

    def forward_some(self, count):
        rest = self.firsts[count:]
        self.firsts = self.firsts[:count]
        self.forward()
        self.firsts = rest

    def arrive(self):
        for copy in self.mates:
            copy.wait_recv()
        self.mates = []


def sems(count):
    return pltpu.SemaphoreType.DMA((count,))


def shape(dims, dtype):
    return jax.ShapeDtypeStruct(tuple(dims), dtype)


def call(kernel, outs, in_specs, out_specs, scratch, cid, name, args, vmem=None):
    return pl.pallas_call(
        kernel,
        out_shape=outs,
        in_specs=in_specs,
        out_specs=out_specs,
        scratch_shapes=scratch,
        compiler_params=pltpu.CompilerParams(
            collective_id=cid, has_side_effects=True, vmem_limit_bytes=vmem
        ),
        name=name,
    )(*args)


def small_sends(dims):
    return dims[0] * dims[1] * dims[2] * 2 - 1


def gather_all(dims, layers, first_axes, table, classes, gains, labels, targets, heights, masks, cid):
    nz, ny, nx = dims
    n = len(layers)
    rows, width = table.shape
    images, local_len = targets.shape
    length = local_len * 2
    columns = gains.shape[1]
    meta = (8, 128)
    count_images = nz * ny * nx * images
    label_rows = -(-count_images // 128)
    groups = [(k,) for k in range(nz)] if nz <= 4 else [tuple(range(nz))]

    def kernel(*refs):
        ins, rest = (refs[:n], refs[n:])
        table_in, class_in, gain_in, labels_in, targets_in, heights_in, masks_in, *rest = rest
        outs, rest = (rest[:n], rest[n:])
        start_out, gain_out, meta_out, allowed_out, *rest = rest
        low, rest = (rest[:n], rest[n:])
        whole, found, total, class_low, gain_row, meta_in, parts_out, small_out, small_in, *rest = rest
        ssem, rsem, lsem = rest
        place = Place(dims)
        z, y, x, c = (place.z, place.y, place.x, place.c)
        chip = (z * ny + y) * nx + x
        meta_in[...] = jnp.zeros_like(meta_in)
        meta_in[0:images] = targets_in[...]
        meta_in[images : 2 * images] = masks_in[...]
        lane = lax.broadcasted_iota(jnp.int32, (1, 128), 1)
        for i in range(images):
            meta_in[4:5] += jnp.where(lane == i, labels_in[i], 0)
            meta_in[4:5] += jnp.where(lane == images + i, heights_in[i], 0)
            for r in range(label_rows):
                meta_in[5 + r : 6 + r] += jnp.where(lane == chip * images + i - 128 * r, labels_in[i], 0)
        greet(place, all_offsets(dims))
        comm = Comm(ssem, rsem, lsem)
        metas = small_exchange(comm, place, lambda *spot: meta_in, meta_out, False)
        meta_out[z, y, x, c] = meta_in[...]
        waits = []
        whole[y, x, c] = table_in[...].astype(BF)
        tables, blocks = (PlaneGather(comm, place), PlaneGather(comm, place))
        for first, start in (("x", 0), ("y", rows // 2)):
            half = pl.ds(start, rows // 2)
            tables.spread(lambda yy, xx, half=half: whole.at[yy, xx, c, half], first)
        for a in range(n):
            low[a][...] = ins[a][...].astype(BF)
        along = {}
        for s in range(1, nz):
            for a in range(n):
                along[s, a] = comm.send(low[a], outs[a].at[z, y, x, c], place.dev(z=s))
        kept = [comm.keep(low[a], outs[a].at[z, y, x, c]) for a in range(n)]

        def spread(group):
            for a in range(n):
                for k in group:
                    if k:
                        along[k, a].wait_recv()
                if len(group) > 1:
                    comm.done(kept[a])
                    at = pl.ds(0, nz)
                else:
                    at = place.zs(group[0])
                blocks.spread(
                    lambda yy, xx, a=a, at=at: outs[a].at[at, yy, xx, c],
                    first_axes[a],
                    low[a] if group == (0,) else None,
                )

        for copy in metas:
            copy.wait_recv()

        class_low[...] = jnp.zeros_like(class_low)
        class_low[0:columns, 0 : class_in.shape[1]] = class_in[...]
        small_in[...] = jnp.zeros_like(small_in)
        for r in range(label_rows):
            labels = jnp.zeros((1, 128), jnp.int32)
            for k in range(nz * ny * nx):
                labels = labels + meta_out[k // (ny * nx), k // nx % ny, k % nx, 0, 5 + r : 6 + r, :]
            pick = lax.broadcasted_iota(jnp.int32, (class_low.shape[1], 128), 0) == labels
            picked = lax.dot_general(
                jnp.where(pick, 1.0, 0.0).astype(BF),
                class_low[...].astype(BF),
                (((0,), (1,)), ((), ())),
                preferred_element_type=F32,
            )
            for i in range(min(128, count_images - 128 * r)):
                k, core = divmod(128 * r + i, 2)
                small_in[k // (ny * nx), k // nx % ny, k % nx, core, 0:1, 0 : class_low.shape[0]] = picked[
                    i : i + 1
                ]
        gain_row[...] = jnp.zeros_like(gain_row)
        gain_row[0:3, 0:columns] = gain_in[...].astype(BF).astype(F32)

        @pl.loop(0, nz)
        def _(k):
            for j in range(ny):
                for i in range(nx):
                    for core in range(2):
                        small_in[k, j, i, core, 1:4, :] = gain_row[0:3]

        smalls = small_exchange(comm, place, lambda *spot: small_in.at[spot], small_out, False)
        small_out[z, y, x, c] = small_in[z, y, x, c]

        size = len(layers)
        steps = [lambda group=group: spread(group) for group in groups]
        steps.pop(0)()
        tables.forward()
        if steps:
            steps.pop(0)()
        blocks.forward_some(size)
        if steps:
            steps.pop(0)()
        tables.settle()
        blocks.forward_some(size)
        for step in steps:
            step()
        tables.arrive()

        for s in range(1, nz + 1):
            zz = place.zs(s % nz)
            halves = []
            for half in range(2):
                codes = meta_out[zz, y, x, half, pl.ds(c, 1), :].astype(F32)
                halves.append(jnp.broadcast_to(codes, (128, local_len)).T)
            column = jnp.concatenate(halves, axis=0)
            column = column - (z * ny * nx * 2 * rows).astype(F32)
            total[...] = jnp.zeros_like(total)

            @pl.loop(0, ny * nx * 2)
            def _(j):
                base = (j * rows).astype(F32)
                lane = lax.broadcasted_iota(jnp.int32, (length, 128), 1).astype(F32) + base
                picks = [
                    jnp.where(column == lane + float(128 * q), 1.0, 0.0).astype(BF)
                    for q in range(-(-rows // 128))
                ]
                pick = jnp.concatenate(picks, axis=1)[:, :rows]
                total[...] += matmul(pick, whole[j // (2 * nx), j // 2 % nx, j % 2])

            found[s % nz] = total[...].astype(BF)
            if s < nz:
                waits.append(comm.send(found.at[s], parts_out.at[nz - s - 1], place.dev(z=nz - s)))
            blocks.forward_some(size)
        blocks.forward()
        height = jnp.where(c == 0, heights_in[0], heights_in[images - 1])
        query = lax.broadcasted_iota(jnp.int32, (length, length), 0)
        key = lax.broadcasted_iota(jnp.int32, (length, length), 1)
        allowed_out[...] = jnp.where((key <= query) & (key < GRID * height), 1.0, 0.0)
        for copy in smalls:
            copy.wait_recv()
        joined = jnp.zeros((8, width), F32)
        blank = jnp.zeros((8, width - 128), F32)
        for d in range(2 * nz * ny * nx):
            k, core = divmod(d, 2)
            piece = small_out[k // (ny * nx), k // nx % ny, k % nx, core]
            joined = joined + pltpu.roll(jnp.concatenate([piece, blank], axis=1), columns * d, 1)
        gain_out[...] = jnp.concatenate([joined[1:4], jnp.zeros((5, width), F32)], axis=0)
        blocks.settle()
        for copy in waits:
            copy.wait_recv()
        added = found[0].astype(F32)
        for s in range(1, nz):
            added = added + parts_out[s - 1].astype(F32)
        first = lax.broadcasted_iota(jnp.int32, (length, 128), 0) == 0
        for k in range(width // 128):
            at = slice(128 * k, 128 * k + 128)
            start_out[:, at] = jnp.where(first, joined[0:1, at], pltpu.roll(added[:, at], 1, 0))
        blocks.arrive()
        comm.finish()

    count = n * (nz - 1) + (n * len(groups) + 2) * (2 * ny * nx - 1) + nz + 2 * small_sends(dims)
    small = dims + (2, 8, 128)
    outs = [shape(dims + (2,) + v.shape, BF) for v in layers]
    outs += [
        shape((length, width), F32),
        shape((8, width), F32),
        shape(dims + (2,) + meta, jnp.int32),
        shape((length, length), F32),
    ]
    scratch = [pltpu.VMEM(v.shape, BF) for v in layers]
    scratch += [
        pltpu.VMEM((ny, nx, 2) + table.shape, BF),
        pltpu.VMEM((nz, length, width), BF),
        pltpu.VMEM((length, width), F32),
        pltpu.VMEM((-(-columns // 16) * 16, -(-classes.shape[1] // 128) * 128), F32),
        pltpu.VMEM((8, 128), F32),
        pltpu.VMEM(meta, jnp.int32),
        pltpu.VMEM((nz - 1, length, width), BF),
        pltpu.VMEM(small, F32),
        pltpu.VMEM(small, F32),
        sems(count),
        sems(count),
        sems(n),
    ]
    return call(
        kernel, outs, [VMEM] * (n + 3) + [SMEM, VMEM, SMEM, VMEM], [ANY] * n + [VMEM] * 4, scratch,
        cid, "gather_all", (*layers, table, classes, gains, labels, targets, heights, masks), 60 * 2**20,
    )


def add_blocks(out, terms):
    lead = out.shape[:-2]

    def visit(index):
        if len(index) < len(lead):

            @pl.loop(0, lead[len(index)])
            def _(i):
                visit(index + (i,))

        else:
            if len(terms) == 2 and out.dtype == BF:
                out[index] = terms[0][index] + terms[1][index]
                return
            total = terms[0][index].astype(F32)
            for term in terms[1:]:
                total = total + term[index].astype(F32)
            out[index] = total.astype(out.dtype)

    visit(())


def items_of(shapes, axes):
    if shapes[0][0] % 8:
        return [[(a, slice(0, shapes[a][0]), slice(0, shapes[a][1]), axes[a]) for a in pair] for pair in ((2, 3), (0, 1))]
    (rows, qkv), (_, mix), (_, both), (deep, width) = shapes
    every, piece = (slice(0, rows), both // 4)
    return [
        [(3, slice(0, deep // 2), slice(0, width), "x"), (3, slice(deep // 2, deep), slice(0, width), "y")],
        [(2, every, slice(0, piece), "x"), (2, every, slice(2 * piece, 3 * piece), "y")],
        [(0, every, slice(0, 2 * mix), "x"), (0, every, slice(2 * mix, qkv), "y"), (1, every, slice(0, mix), "y")],
        [(2, every, slice(piece, 2 * piece), "x"), (2, every, slice(3 * piece, both), "y")],
    ]


def scatter_all(dims, grads, axes, rows, gains, metas, head, partial, device_codes, classes, cid):
    nz, ny, nx = dims
    plane = ny * nx
    n = len(grads)
    shapes = [g.shape[4:] for g in grads]
    steps = items_of(shapes, axes)
    items = [item for step in steps for item in step]
    order, at = ([], 0)
    for step in steps:
        order.append(list(range(at, at + len(step))))
        at += len(step)
    length, width = rows.shape
    block = (device_codes, width)
    sizes = {"x": nx, "y": ny}
    columns = width // (2 * nz * plane)
    label_rows = -(-2 * nz * plane // 128)

    def kernel(*refs):
        parts, rest = (refs[:n], list(refs[n:]))
        rows_in, gains_in, meta_in, head_in, partial_in = (rest.pop(0) for _ in range(5))
        outs = [rest.pop(0) for _ in range(n)]
        table_out, class_out, gain_out, sums = (rest.pop(0) for _ in range(4))
        owns, halves, ones, twos, threes = ([rest.pop(0) for _ in items] for _ in range(5))
        near, far = ([rest.pop(0), rest.pop(0)] for _ in range(2))
        lined, given, own, half, small_in, small_out, tops, mine, every, ssem, rsem, lsem = rest
        place = Place(dims)
        z, y, x, c = (place.z, place.y, place.x, place.c)
        comm = Comm(ssem, rsem, lsem)
        kept = []
        for i, (a, span, cols, _) in enumerate(items):
            kept.append(comm.keep(parts[a].at[:, :, :, c, span, cols], owns[i]))
        lane = lax.broadcasted_iota(jnp.int32, (8, 128), 1)
        top = jnp.concatenate([rows_in[0:1], gains_in[0:3], jnp.zeros((4, width), F32)], axis=0)
        for d in range(2 * nz * plane):
            k, core = divmod(d, 2)
            piece = pltpu.roll(top, (width - columns * d) % width, 1)[:, :128]
            small_in[k // plane, k // nx % ny, k % nx, core] = jnp.where(lane < columns, piece, 0.0)
        greet(place, all_offsets(dims))
        waits = small_exchange(comm, place, lambda *spot: small_in.at[spot], small_out, False)
        small_out[z, y, x, c] = small_in[z, y, x, c]
        pair, got_one, got_two, third = ({}, {}, {}, {})

        def set_out(g):
            for i in order[g] if g < len(order) else []:
                a, span, cols, _ = items[i]
                pair[i] = comm.send(parts[a].at[:, :, :, 1 - c, span, cols], halves[i], place.dev(c=1))

        def back(axis, t):
            return place.ys(ny - t) if axis == "y" else place.xs(nx - t)

        def first_add(g):
            for i in order[g]:
                pair[i].wait_recv()
                comm.done(kept[i])
                add_blocks(halves[i], [halves[i], owns[i]])

        def first_send(g):
            for i in order[g]:
                axis = items[i][3]
                got_one[i] = [
                    comm.send(
                        halves[i].at[:, back(axis, t)] if axis == "y" else halves[i].at[:, :, back(axis, t)],
                        ones[i].at[t - 1],
                        place.dev(**{axis: t}),
                    )
                    for t in range(1, sizes[axis])
                ]

        def second_step(g):
            for i in order[g]:
                axis = items[i][3]
                other = "x" if axis == "y" else "y"
                for copy in got_one[i]:
                    copy.wait_recv()
                held = halves[i].at[:, y] if axis == "y" else halves[i].at[:, :, x]
                add_blocks(held, [held] + [ones[i].at[t] for t in range(ones[i].shape[0])])
                got_two[i] = [
                    comm.send(
                        halves[i].at[:, y, back("x", t)] if other == "x" else halves[i].at[:, back("y", t), x],
                        twos[i].at[t - 1],
                        place.dev(**{other: t}),
                    )
                    for t in range(1, sizes[other])
                ]

        def third_step(g):
            for i in order[g]:
                for copy in got_two[i]:
                    copy.wait_recv()
                held = halves[i].at[:, y, x]
                add_blocks(held, [held] + [twos[i].at[t] for t in range(twos[i].shape[0])])
                third[i] = [
                    comm.send(halves[i].at[place.zs(nz - s), y, x], threes[i].at[s - 1], place.dev(z=s))
                    for s in range(1, nz)
                ]

        def last_step(g):
            for i in order[g]:
                a, span, cols, _ = items[i]
                for copy in third[i]:
                    copy.wait_recv()
                terms = [halves[i].at[z, y, x]] + [threes[i].at[s] for s in range(nz - 1)]
                add_blocks(outs[a].at[span, cols], terms)

        flat = []
        first = lax.broadcasted_iota(jnp.int32, (1, length), 1) == 0
        for s in range(nz):
            codes = [meta_in[place.zs(s), y, x, part, pl.ds(c, 1), :] for part in range(2)]
            codes = pltpu.roll(jnp.concatenate(codes, axis=1) - z * (2 * plane * device_codes), 1, 1)
            flat.append(jnp.where(first, -1, codes))
        flat = jnp.concatenate(flat, axis=1)

        def product(into, core):
            @pl.loop(0, plane)
            def _(j):
                code = lax.broadcasted_iota(jnp.int32, (device_codes, nz * length), 0)
                pick = code + (j * 2 + core) * device_codes == flat
                pick = jnp.where(pick, 1.0, 0.0).astype(BF)
                value = matmul(pick, lined[...].reshape(nz * length, width))
                into[j // nx, j % nx] = value.astype(BF)

        set_out(0)
        set_out(1)
        lined[0] = rows_in[...].astype(BF)
        lines = [comm.send(lined.at[0], lined.at[s], place.dev(z=s)) for s in range(1, nz)]
        count = len(order)
        for g in range(count):
            first_add(g)
            set_out(g + 2)
            if g >= 2:
                second_step(g - 2)
            first_send(g)
            if g >= 3:
                third_step(g - 3)
        for copy in lines:
            copy.wait_recv()
        product(given, 1 - c)
        table_pair = comm.send(given, half, place.dev(c=1))
        second_step(count - 2)
        product(own, c)
        if count > 2:
            third_step(count - 3)
        second_step(count - 1)
        table_pair.wait_recv()
        add_blocks(half, [half, own])
        parts_of = [pl.ds(0, device_codes // 2), pl.ds(device_codes // 2, device_codes // 2)]
        came = [
            [
                comm.send(half.at[:, back("x", t), parts_of[0]], near[0].at[t - 1], place.dev(x=t))
                for t in range(1, nx)
            ],
            [
                comm.send(half.at[back("y", t), :, parts_of[1]], near[1].at[t - 1], place.dev(y=t))
                for t in range(1, ny)
            ],
        ]
        third_step(count - 2)
        third_step(count - 1)

        for copy in waits:
            copy.wait_recv()
        gain_out[...] = jnp.zeros_like(gain_out)
        tops[...] = jnp.zeros_like(tops)

        @pl.loop(0, nz)
        def _(k):
            for j in range(ny):
                for i in range(nx):
                    for core in range(2):
                        at = ((k * ny + j) * nx + i) * 2 + core
                        tops[pl.ds(at, 1), :] = small_out[k, j, i, core, 0:1, :]
                        gain_out[...] += small_out[k, j, i, core]

        value = jnp.zeros(class_out.shape, F32)
        high = class_out.shape[1]
        for r in range(label_rows):
            labels = jnp.zeros((1, 128), jnp.int32)
            for k in range(nz * plane):
                labels = labels + meta_in[k // plane, k // nx % ny, k % nx, 0, 5 + r : 6 + r, :]
            at = lax.broadcasted_iota(jnp.int32, (high, 128), 1) + 128 * r
            pick = lax.broadcasted_iota(jnp.int32, (high, 128), 0) == labels
            pick = jnp.where(pick & (at < 2 * nz * plane), 1.0, 0.0)
            value = value + lax.dot_general(
                tops[128 * r : 128 * r + 128],
                pick,
                (((0,), (1,)), ((), ())),
                precision=lax.Precision.HIGHEST,
                preferred_element_type=F32,
            )
        class_out[...] = value
        row = lax.broadcasted_iota(jnp.int32, gain_out.shape, 0)
        gained = jnp.where((row >= 1) & (row < 4), gain_out[...], 0.0)
        square = jnp.sum(value * value) + jnp.sum(gained * gained)
        share = head_in[...].astype(F32)
        square = square + jnp.sum(share * share)
        for g in range(count - 1):
            last_step(g)

        for copy in came[0] + came[1]:
            copy.wait_recv()
        for h, held in ((0, half.at[:, x, parts_of[0]]), (1, half.at[y, :, parts_of[1]])):
            add_blocks(held, [held] + [near[h].at[t] for t in range(near[h].shape[0])])
        came = [
            comm.send(half.at[back("y", t), x, parts_of[0]], far[0].at[t - 1], place.dev(y=t))
            for t in range(1, ny)
        ]
        came += [
            comm.send(half.at[y, back("x", t), parts_of[1]], far[1].at[t - 1], place.dev(x=t))
            for t in range(1, nx)
        ]
        last_step(count - 1)
        for a in range(n):
            square = square + jnp.sum(outs[a][...] * outs[a][...])
        for copy in came:
            copy.wait_recv()
        for h in range(2):
            terms = [half.at[y, x, parts_of[h]]] + [far[h].at[t] for t in range(far[h].shape[0])]
            add_blocks(table_out.at[parts_of[h]], terms)
        square = square + jnp.sum(table_out[...] * table_out[...])
        first = (lax.broadcasted_iota(jnp.int32, mine.shape, 0) == 0) & (
            lax.broadcasted_iota(jnp.int32, mine.shape, 1) == 0
        )
        mine[...] = partial_in[...] + jnp.where(first, square, 0.0)
        for copy in small_exchange(comm, place, lambda *spot: mine, every, False):
            copy.wait_recv()
        every[z, y, x, c] = mine[...]
        sums[...] = jnp.zeros_like(sums)

        @pl.loop(0, nz)
        def _(k):
            for j in range(ny):
                for i in range(nx):
                    sums[...] += every[k, j, i, 0] + every[k, j, i, 1]

        comm.finish()

    total = len(items) * (ny + nx - 1 + nz - 1) + nz + 2 * (ny + nx) + 2 * small_sends(dims)
    cuts = [(span.stop - span.start, cols.stop - cols.start) for _, span, cols, _ in items]
    near_far = [(ny, nx) if item[3] == "y" else (nx, ny) for item in items]
    part = (device_codes // 2, width)
    scratch = [pltpu.VMEM((nz, ny, nx) + t, BF) for t in cuts] * 2
    scratch += [pltpu.VMEM((u - 1, nz, v) + t, BF) for t, (u, v) in zip(cuts, near_far)]
    scratch += [pltpu.VMEM((v - 1, nz) + t, BF) for t, (u, v) in zip(cuts, near_far)]
    scratch += [pltpu.VMEM((nz - 1,) + t, BF) for t in cuts]
    scratch += [
        pltpu.VMEM((nx - 1, ny) + part, BF),
        pltpu.VMEM((ny - 1, nx) + part, BF),
        pltpu.VMEM((ny - 1,) + part, BF),
        pltpu.VMEM((nx - 1,) + part, BF),
        pltpu.VMEM((nz, length, width), BF),
        pltpu.VMEM((ny, nx) + block, BF),
        pltpu.VMEM((ny, nx) + block, BF),
        pltpu.VMEM((ny, nx) + block, BF),
        pltpu.VMEM(dims + (2, 8, 128), F32),
        pltpu.VMEM(dims + (2, 8, 128), F32),
        pltpu.VMEM((128 * label_rows, 128), F32),
        pltpu.VMEM(partial.shape, F32),
        pltpu.VMEM(dims + (2,) + partial.shape, F32),
        sems(total),
        sems(total),
        sems(len(items)),
    ]
    outs = [shape(t, F32) for t in shapes]
    high = -(-classes // 128) * 128
    outs += [shape(block, F32), shape((128, high), F32), shape((8, 128), F32), shape(partial.shape, F32)]
    return call(
        kernel, outs, [ANY] * n + [VMEM] * 5, [VMEM] * (n + 4), scratch,
        cid, "scatter_all", (*grads, rows, gains, metas, head, partial), 60 * 2**20,
    )


def head_all(dims, middle, gain, metas, head, expand_w, shrink_w, images, cid):
    nz, ny, nx = dims
    length, width = middle.shape
    inner = shrink_w.shape[0]
    pieces = inner // PIECE
    columns = head.shape[1]
    lanes = min(columns, 128)
    groups = columns // lanes
    plane = ny * nx
    blocks = 2 * plane
    keep = columns >= 128
    shared = columns == PIECE and nz * length >= width and blocks >= 2 * pieces

    def kernel(*refs):
        middle_in, gain_in, meta_in, head_in, expand_in, shrink_in, *rest = refs
        top_out, head_out, loss_out, both_out, final_out, *rest = rest
        whole, marks_in, wide, lined, turned, peaks, totals, picks, exps, grads, *rest = rest
        columned, partial, back, coming, mine, every, given, half, ssem, rsem, lsem = rest
        place = Place(dims)
        z, y, x, c = (place.z, place.y, place.x, place.c)
        greet(place, line_offsets(dims))
        comm = Comm(ssem, rsem, lsem)
        room, loads = ({}, {})

        def load(j):
            room[j] = grads.at[j, pl.ds(0, width)] if shared else wide.at[j // pieces]
            loads[j] = comm.keep(expand_in.at[:, pl.ds(PIECE * j, PIECE)], room[j])

        for j in range(2 * pieces) if shared else []:
            load(j)
        whole[c, y, x] = head_in[...].astype(BF)
        gather = PlaneGather(comm, place)
        for first, start in (("x", 0), ("y", width // 2)):
            part = pl.ds(start, width // 2)
            gather.spread(lambda yy, xx, part=part: whole.at[c, yy, xx, part], first)
        normed = norm_forward(middle_in[...], gain_in[1:2])[0].astype(BF)
        total = middle_in[...]
        for j in range(pieces):
            at = slice(PIECE * j, PIECE * (j + 1))
            for k in (j, pieces + j):
                if not shared:
                    load(k)
                comm.done(loads[k])
            gate, up = (matmul(normed, room[j][...]), matmul(normed, room[pieces + j][...]))
            both_out[:, at] = gate
            both_out[:, inner + PIECE * j : inner + PIECE * (j + 1)] = up
            hidden = (gate * jax.nn.sigmoid(gate) * up).astype(BF)
            total = total + matmul(hidden, shrink_in[at])
        final_out[...] = total
        lined[0] = norm_forward(total, gain_in[2:3])[0].astype(BF)
        turns = sorted(range(1, nz), key=lambda s: min(s, nz - s))
        arriving = {s: comm.send(lined.at[0], lined.at[s], place.dev(z=s)) for s in turns[:2]}
        turned[:, 0:length] = lined[0].T
        for s in range(nz):
            for part in range(2):
                codes = meta_in[place.zs(s), y, x, part, pl.ds(c, 1), :].astype(F32)
                tall = jnp.broadcast_to(codes, (128, 128)).T.astype(jnp.int32)
                marks_in[s, 128 * part : 128 * part + 128] = tall[:, :lanes] - z * (blocks * columns)
        gather.forward()
        gather.settle()
        for s in turns[:2]:
            comm.gone(arriving[s])
        for s in turns[2:]:
            arriving[s] = comm.send(lined.at[0], lined.at[s], place.dev(z=s))
        gather.arrive()

        def block(k):
            return whole[k // plane, k // nx % ny, k % nx]

        def split(value):
            return [value[:, lanes * q : lanes * (q + 1)] for q in range(groups)]

        def hits(s, k):
            base = (k % plane * 2 + k // plane) * columns
            lane = lax.broadcasted_iota(jnp.int32, (length, lanes), 1) + base
            return [lane + lanes * q == marks_in[s] for q in range(groups)]

        def logits_of(s, k):
            return matmul(lined[s], block(k))

        def forward(s):
            at = pl.ds(s * length, length)
            peaks[...] = jnp.full_like(peaks, -jnp.inf)
            totals[...] = jnp.zeros_like(totals)
            picks[...] = jnp.zeros_like(picks)

            @pl.loop(0, blocks)
            def _(k):
                logits = logits_of(s, k)
                if keep:
                    exps[k, at] = logits
                high, found = (peaks[...], picks[...])
                for piece, hit in zip(split(logits), hits(s, k)):
                    high = jnp.maximum(high, piece)
                    found = found + jnp.where(hit, piece, 0.0)
                peaks[...] = high
                picks[...] = found

            peak = jnp.max(peaks[...], axis=1, keepdims=True)
            peaks[...] = jnp.broadcast_to(peak, (length, lanes))

            @pl.loop(0, blocks)
            def _(k):
                logits = exps[k, at] if keep else logits_of(s, k)
                total = totals[...]
                for q, piece in enumerate(split(logits)):
                    power = jnp.exp(piece - peaks[...])
                    if keep:
                        exps[k, at, lanes * q : lanes * (q + 1)] = power
                    total = total + power
                totals[...] = total

            if not keep:
                exps[s] = peaks[...]
            lane = lax.broadcasted_iota(jnp.int32, (length, 128), 1)
            total = jnp.sum(totals[...], axis=1, keepdims=True)
            found = jnp.sum(picks[...], axis=1, keepdims=True)
            table = jnp.where(lane == 0, peak, jnp.where(lane == 1, total, found))
            mine[place.zs(s)] = table.T[:8]

        forward(0)
        for s in turns:
            arriving[s].wait_recv()
            turned[:, s * length : (s + 1) * length] = lined[s].T
            forward(s)
        stats = [comm.send(mine, every.at[s], place.dev(z=s)) for s in range(1, nz)]
        every[0] = mine[...]
        for copy in stats:
            copy.wait_recv()

        def backward(s):
            at = pl.ds(s * length, length)
            held = [every[q, place.zs(s)] for q in range(nz)]
            peak = held[0][0:1]
            for other in held[1:]:
                peak = jnp.maximum(peak, other[0:1])
            total = sum(other[1:2] * jnp.exp(other[0:1] - peak) for other in held)
            zz = place.zs(s)
            mask = [meta_in[zz, y, x, part, pl.ds(images + c, 1), :] for part in range(2)]
            mask = jnp.concatenate(mask, axis=1).astype(F32)
            tail = meta_in[zz, y, x, 0, 4:5, :]
            lane = lax.broadcasted_iota(jnp.int32, (1, 128), 1)
            tall = jnp.sum(jnp.where(lane == images + c, tail, 0).astype(F32), axis=1, keepdims=True)
            place_of = lax.broadcasted_iota(jnp.int32, (1, length), 1).astype(F32)
            weight = jnp.where(place_of < GRID * tall, mask, 0.0)
            if s == 0:
                found = sum(other[2:3] for other in held)
                loss = (peak + jnp.log(total) - found) * weight
                lane = lax.broadcasted_iota(jnp.int32, (8, 128), 1)
                row = lax.broadcasted_iota(jnp.int32, (8, 128), 0)
                sums = jnp.where(lane == 1, jnp.sum(loss, axis=1, keepdims=True), 0.0)
                sums = sums + jnp.where(lane == 2, jnp.sum(weight, axis=1, keepdims=True), 0.0)
                loss_out[...] = jnp.where(row == 0, sums, 0.0)
            scale = weight / total * jnp.exp(held[0][0:1] - peak)
            tall = jnp.concatenate([scale, weight, jnp.zeros((126, length), F32)], axis=0).T
            columned[0] = jnp.broadcast_to(tall[:, 0:1], (length, lanes))
            columned[1] = jnp.broadcast_to(tall[:, 1:2], (length, lanes))
            partial[...] = jnp.zeros_like(partial)

            @pl.loop(0, blocks)
            def _(k):
                if keep:
                    powers = split(exps[k, at])
                else:
                    powers = [jnp.exp(piece - exps[s]) for piece in split(logits_of(s, k))]
                pieces = []
                for power, hit in zip(powers, hits(s, k)):
                    grad = power * columned[0] - jnp.where(hit, columned[1], 0.0)
                    pieces.append(grad.astype(BF))
                grad = jnp.concatenate(pieces, axis=1) if groups > 1 else pieces[0]
                grads[k, at] = grad
                partial[...] += lax.dot_general(
                    grad, block(k), (((1,), (1,)), ((), ())), preferred_element_type=F32
                )

        coming_in = []
        for s in range(1, nz):
            backward(s)
            back[s - 1] = partial[...].astype(BF)
            coming_in.append(comm.send(back.at[s - 1], coming.at[s - 1], place.dev(z=nz - s)))
        backward(0)

        def weights(into, core):
            @pl.loop(0, plane)
            def _(j):
                into[j // nx, j % nx] = matmul(turned[...], grads[core * plane + j]).astype(BF)

        weights(given, 1 - c)
        pair = comm.send(given, half, place.dev(c=1))
        weights(head_out, c)
        pair.wait_recv()
        add_blocks(head_out, [head_out, half])
        for copy in coming_in:
            copy.wait_recv()
        total = partial[...]
        for s in range(nz - 1):
            total = total + coming[s].astype(F32)
        top_out[...] = total
        comm.finish()

    count = 3 * (nz - 1) + 2 * (2 * plane - 1) + 1
    scratch = [
        pltpu.VMEM((2, ny, nx) + head.shape, BF),
        pltpu.VMEM((nz, length, lanes), jnp.int32),
        pltpu.VMEM((16, 128) if shared else (2, width, PIECE), BF),
        pltpu.VMEM((nz, length, width), BF),
        pltpu.VMEM((width, nz * length), BF),
        pltpu.VMEM((length, lanes), F32),
        pltpu.VMEM((length, lanes), F32),
        pltpu.VMEM((length, lanes), F32),
        pltpu.VMEM((blocks, nz * length, columns) if keep else (nz, length, lanes), F32),
        pltpu.VMEM((blocks, nz * length, columns), BF),
        pltpu.VMEM((2, length, lanes), F32),
        pltpu.VMEM((length, width), F32),
        pltpu.VMEM((nz - 1, length, width), BF),
        pltpu.VMEM((nz - 1, length, width), BF),
        pltpu.VMEM((nz, 8, length), F32),
        pltpu.VMEM((nz, nz, 8, length), F32),
        pltpu.VMEM((ny, nx) + head.shape, BF),
        pltpu.VMEM((ny, nx) + head.shape, BF),
        sems(count),
        sems(count),
        sems(2 * pieces),
    ]
    outs = [
        shape((length, width), F32),
        shape((ny, nx) + head.shape, BF),
        shape((8, 128), F32),
        shape((length, 2 * inner), F32),
        shape((length, width), F32),
    ]
    return call(
        kernel, outs, [VMEM] * 4 + [ANY, VMEM], [VMEM] * 5, scratch,
        cid, "head_all", (middle, gain, metas, head, expand_w, shrink_w), 63 * 2**20,
    )


def matmul(left, right):
    return jnp.dot(left, right, preferred_element_type=F32)


def norm_forward(values, gain):
    inverse = lax.rsqrt(jnp.mean(values * values, axis=-1, keepdims=True) + EPS_NORM)
    normed = values * inverse
    return (normed * gain, normed, inverse)


def norm_backward(grad, normed, inverse, gain):
    scaled = grad * gain
    inner = jnp.mean(scaled * normed, axis=-1, keepdims=True)
    return (inverse * (scaled - normed * inner), jnp.sum(grad * normed, axis=0))


def turned(value, low):
    return jnp.where(low, -pltpu.roll(value, 112, 1), pltpu.roll(value, 16, 1))


def low_quarters(rows):
    return lax.broadcasted_iota(jnp.int32, (rows, 128), 1) % 32 < 16


def left_half(rows):
    return lax.broadcasted_iota(jnp.int32, (rows, 128), 1) < HD


def times_turned(left, right):
    return lax.dot_general(left, right, (((1,), (1,)), ((), ())), preferred_element_type=F32)


def turned_times(left, right):
    return lax.dot_general(left, right, (((0,), (0,)), ((), ())), preferred_element_type=F32)


def attention_steps(start, gain, angles, allowed, weights, mix, held, probs, out):
    length, width = start.shape
    normed = norm_forward(start[...], gain[0:1])[0].astype(BF)
    low, left = (low_quarters(length), left_half(length))
    for k in range(3):
        value = matmul(normed, weights(k))
        for p in range(width // 128):
            piece = value[:, 128 * p : 128 * p + 128]
            if k < 2:
                piece = piece * angles[0] + turned(piece, low) * angles[1]
            held[k, :, 128 * p : 128 * p + 128] = piece.astype(BF)
        yield
    for p in range(width // 128):
        at = slice(128 * p, 128 * p + 128)
        query, keys, values = (held[0, :, at], held[1, :, at], held[2, :, at])
        parts = []
        for side in range(2):
            own = jnp.where(left == (side == 0), query, jnp.zeros_like(query))
            scores = times_turned(own, keys) * HD ** (-0.5)
            scores = jnp.where(allowed[...] > 0, scores, NEGATIVE_FILL)
            power = jnp.exp(scores - jnp.max(scores, axis=1, keepdims=True))
            power = power / jnp.sum(power, axis=1, keepdims=True)
            probs[2 * p + side] = power
            parts.append(matmul(power.astype(BF), values))
        held[3, :, at] = jnp.where(left, parts[0], parts[1]).astype(BF)
        yield
    out[...] = start[...] + matmul(held[3], mix())
    yield


def attention_back_steps(start, gain, angles, weights, mix, held, probs, grad_mid, put, out, gains):
    length, width = start.shape
    low, left = (low_quarters(length), left_half(length))
    back = grad_mid[...].astype(BF)
    put(3, turned_times(held[3], back))
    grad_out = times_turned(back, mix()).astype(BF)
    yield
    grads = [[], [], []]
    for p in range(width // 128):
        at = slice(128 * p, 128 * p + 128)
        query, keys, values, grad = (held[0, :, at], held[1, :, at], held[2, :, at], grad_out[:, at])
        parts = []
        for side in range(2):
            own = jnp.where(left == (side == 0), grad, jnp.zeros_like(grad))
            grad_probs = times_turned(own, values)
            power = probs[2 * p + side]
            inner = jnp.sum(power * grad_probs, axis=1, keepdims=True)
            score = (power * (grad_probs - inner)).astype(BF)
            parts.append(
                (
                    matmul(score, keys) * HD ** (-0.5),
                    turned_times(score, query) * HD ** (-0.5),
                    turned_times(power.astype(BF), grad),
                )
            )
        for k in range(3):
            value = jnp.where(left, parts[0][k], parts[1][k]).astype(BF)
            if k < 2:
                value = value.astype(F32)
                value = (value * angles[0] - turned(value * angles[1], low)).astype(BF)
            grads[k].append(value)
        yield
    gain_row = gain[0:1]
    normed_gain, normed, inverse = norm_forward(start[...], gain_row)
    normed_gain = normed_gain.astype(BF)
    total = jnp.zeros((length, width), F32)
    for k in range(3):
        grad = jnp.concatenate(grads[k], axis=1)
        put(k, turned_times(normed_gain, grad))
        total = total + times_turned(grad, weights(k))
        yield
    grad, gain_grad = norm_backward(total, normed, inverse, gain_row)
    gains[0:1] = gain_grad.reshape(1, width)
    out[...] = grad_mid[...] + grad
    yield


def local_call(kernel, outs, args, scratch, name, flops, spaces=None):
    spaces = [VMEM] * len(args) if spaces is None else spaces
    return pl.pallas_call(
        kernel,
        out_shape=outs,
        in_specs=spaces,
        out_specs=[VMEM] * len(outs),
        scratch_shapes=scratch,
        compiler_params=pltpu.CompilerParams(vmem_limit_bytes=60 * 2**20),
        cost_estimate=pl.CostEstimate(flops=flops, bytes_accessed=2**24, transcendentals=0),
        name=name,
    )(*args)


def attention_forward(start, gain, angles, allowed, qkv_w, mix_w):
    length, width = start.shape

    def kernel(start, gain, angles, allowed, qkv, mix, held, probs, out):
        def weights(k):
            return qkv[:, width * k : width * (k + 1)]

        drain(attention_steps(start, gain, angles, allowed, weights, lambda: mix[...], held, probs, out))

    outs = [
        shape((4, length, width), BF),
        shape((width // HD, length, length), F32),
        shape((length, width), F32),
    ]
    args = (start, gain, angles, allowed, qkv_w, mix_w)
    return local_call(kernel, outs, args, [], "attention_forward", 2**31)


def feed_back_steps(grad_top, final, middle, both, gain, expand, shrink, grad_expand, grad_shrink, out, gains):
    length, width = middle.shape
    inner = shrink.shape[0]
    _, normed, inverse = norm_forward(final[...], gain[2:3])
    grad_final, gain_top = norm_backward(grad_top[...], normed, inverse, gain[2:3])
    back = grad_final.astype(BF)
    low, normed, inverse = norm_forward(middle[...], gain[1:2])
    low = low.astype(BF)
    total = jnp.zeros((length, width), F32)
    for k in range(inner // PIECE):
        at = slice(PIECE * k, PIECE * (k + 1))
        up_at = slice(inner + PIECE * k, inner + PIECE * (k + 1))
        gate, up = (both[:, at], both[:, up_at])
        sigma = jax.nn.sigmoid(gate)
        hidden = (gate * sigma * up).astype(BF)
        grad_shrink[at] = turned_times(hidden, back).astype(BF)
        grad = times_turned(back, shrink[at])
        grad_gate = (grad * up * sigma * (1.0 + gate * (1.0 - sigma))).astype(BF)
        grad_up = (grad * gate * sigma).astype(BF)
        grad_expand[:, at] = turned_times(low, grad_gate).astype(BF)
        grad_expand[:, up_at] = turned_times(low, grad_up).astype(BF)
        total = total + times_turned(grad_gate, expand[:, at])
        total = total + times_turned(grad_up, expand[:, up_at])
        yield
    grad_middle, gain_two = norm_backward(total, normed, inverse, gain[1:2])
    out[...] = grad_final + grad_middle
    gains[...] = jnp.zeros_like(gains)
    gains[1:2] = gain_two.reshape(1, width)
    gains[2:3] = gain_top.reshape(1, width)
    yield


def layer_backward(dims, grad_top, final, middle, both, gain, expand_w, shrink_w, start, angles, attention, head, cid):
    nz, ny, nx = dims
    length, width = middle.shape
    deep, columns = head.shape[2:]
    later = len(attention)

    def kernel(*refs):
        grad_top, final, middle, both, gain, expand, shrink, start, angles, head_in, *rest = refs
        sources, rest = (rest[:later], rest[later:])
        expand_out, shrink_out, grad_qkv, grad_mix, start_out, gains, head_out, *rest = rest
        qkv, mix, held, probs, *rest = rest
        grad_expand, grad_shrink, grad_mid, *rest = rest
        near, mids, fars, (ssem, rsem, lsem) = (rest[0:2], rest[2:4], rest[4:6], rest[6:])
        place = Place(dims)
        y, x = (place.y, place.x)
        comm = Comm(ssem, rsem, lsem)
        loads = [comm.keep(src, dst) for src, dst in zip(sources, (qkv, mix, held, probs))]
        greet(place, [off for off in line_offsets(dims) if off[1] or off[2]])
        parts = (pl.ds(0, deep // 2), pl.ds(deep // 2, deep // 2))
        by_x = [(t, place.xs(nx - t), place.dev(x=t)) for t in range(1, nx)]
        by_y = [(t, place.ys(ny - t), place.dev(y=t)) for t in range(1, ny)]
        came = [comm.send(head_in.at[:, to, parts[0]], near[0].at[t - 1], dev) for t, to, dev in by_x]
        came += [comm.send(head_in.at[to, :, parts[1]], near[1].at[t - 1], dev) for t, to, dev in by_y]
        drain(
            feed_back_steps(
                grad_top, final, middle, both, gain, expand, shrink, grad_expand, grad_shrink, grad_mid, gains
            )
        )
        comm.keep(grad_expand, expand_out)
        comm.keep(grad_shrink, shrink_out)
        for copy in came:
            copy.wait_recv()
        add_blocks(mids[0], [head_in.at[:, x, parts[0]]] + [near[0].at[t] for t in range(nx - 1)])
        add_blocks(mids[1], [head_in.at[y, :, parts[1]]] + [near[1].at[t] for t in range(ny - 1)])
        came = [comm.send(mids[0].at[to], fars[0].at[t - 1], dev) for t, to, dev in by_y]
        came += [comm.send(mids[1].at[to], fars[1].at[t - 1], dev) for t, to, dev in by_x]
        for copy in loads:
            comm.done(copy)

        def weights(k):
            return qkv[:, width * k : width * (k + 1)]

        def put(k, value):
            if k == 3:
                grad_mix[...] = value.astype(BF)
            else:
                grad_qkv[:, width * k : width * (k + 1)] = value.astype(BF)

        drain(
            attention_back_steps(
                start, gain, angles, weights, lambda: mix[...], held, probs, grad_mid, put, start_out, gains
            )
        )
        for copy in came:
            copy.wait_recv()
        for part, mid, far in ((parts[0], mids[0].at[y], fars[0]), (parts[1], mids[1].at[x], fars[1])):
            add_blocks(head_out.at[part], [mid] + [far.at[t] for t in range(far.shape[0])])
        comm.finish()

    count = 2 * (ny + nx)
    half = (deep // 2, columns)
    outs = [
        shape(expand_w.shape, BF),
        shape(shrink_w.shape, BF),
        shape(attention[0].shape, BF),
        shape(attention[1].shape, BF),
        shape((length, width), F32),
        shape((8, width), F32),
        shape(head.shape[2:], F32),
    ]
    scratch = [pltpu.VMEM(v.shape, v.dtype) for v in attention]
    scratch += [pltpu.VMEM(expand_w.shape, BF), pltpu.VMEM(shrink_w.shape, BF)]
    scratch += [
        pltpu.VMEM((length, width), F32),
        pltpu.VMEM((nx - 1, ny) + half, BF),
        pltpu.VMEM((ny - 1, nx) + half, BF),
        pltpu.VMEM((ny,) + half, BF),
        pltpu.VMEM((nx,) + half, BF),
        pltpu.VMEM((ny - 1,) + half, BF),
        pltpu.VMEM((nx - 1,) + half, BF),
        sems(count),
        sems(count),
        sems(later + 2),
    ]
    args = (grad_top, final, middle, both, gain, expand_w, shrink_w, start, angles, head, *attention)
    return call(
        kernel, outs, [VMEM] * 10 + [ANY] * later, [ANY] * 2 + [VMEM] * 5, scratch,
        cid, "layer_backward", args, 60 * 2**20,
    )


def rope_tables(length, width):
    quarter = width // 4
    places = np.arange(length)
    freq = np.float32(10000.0) ** (-np.arange(quarter, dtype=np.float32) / np.float32(quarter))
    row_angle = (places // GRID).astype(np.float32)[:, None] * freq
    col_angle = (places % GRID).astype(np.float32)[:, None] * freq
    angles = np.concatenate([row_angle, row_angle, col_angle, col_angle] * (128 // width), axis=-1)
    return jnp.asarray(np.stack([np.cos(angles), np.sin(angles)]).astype(np.float32))


def adam_update(master, drift, square, grad, rate, decay):
    moment = BETA_ONE * drift + (1.0 - BETA_ONE) * grad
    second = BETA_TWO * square + (1.0 - BETA_TWO) * grad * grad
    stride = (
        moment / (1.0 - BETA_ONE**STEP) / (jnp.sqrt(second / (1.0 - BETA_TWO**STEP)) + ADAM_EPS)
    )
    return (master - rate * (stride + decay * master), moment, second)


def adam_all(masters, drifts, squares, grads, sums, rates, decays):
    n = len(masters)
    pieces = []
    for i, master in enumerate(masters):
        rows = master.shape[0]
        cut = rows // 4 if rows % 32 == 0 and rows >= 256 else rows
        pieces += [(i, k, min(cut, rows)) for k in range(0, rows, cut)]

    def kernel(*refs):
        ins = [refs[n * k : n * (k + 1)] for k in range(4)]
        sums_in = refs[4 * n]
        outs = [refs[4 * n + 1 + n * k : 4 * n + 1 + n * (k + 1)] for k in range(3)]
        sums_out = refs[7 * n + 1]
        rest = refs[7 * n + 2 :]
        held = [rest[n * k : n * (k + 1)] for k in range(4)]
        in_sems, out_sems = rest[4 * n :]
        loads, stores = ([], [])
        for p, (i, at, size) in enumerate(pieces):
            span = pl.ds(at, size)
            loads.append(
                [
                    pltpu.make_async_copy(ins[k][i].at[span], held[k][i].at[span], in_sems.at[p, k])
                    for k in range(4)
                ]
            )
            for copy in loads[-1]:
                copy.start()
        row = sums_in[0:1]
        norm = jnp.sqrt(row[:, 0:1]) / row[:, 2:3]
        factor = CLIP_NORM / jnp.maximum(norm, CLIP_NORM) / row[:, 2:3]
        lane = lax.broadcasted_iota(jnp.int32, (8, 128), 1)
        sums_out[...] = jnp.where(lane == 0, norm, sums_in[...])

        def update(i, span):
            fresh, moment, second = adam_update(
                held[0][i][span],
                held[1][i][span],
                held[2][i][span],
                held[3][i][span] * factor,
                rates[i],
                decays[i],
            )
            held[0][i][span], held[1][i][span], held[2][i][span] = (fresh, moment, second)

        for p, (i, at, size) in enumerate(pieces):
            for copy in loads[p]:
                copy.wait()
            if size % 8:
                update(i, slice(at, at + size))
            else:

                @pl.loop(0, size // 8)
                def _(k, i=i, at=at):
                    update(i, pl.ds(pl.multiple_of(at + 8 * k, 8), 8))

            span = pl.ds(at, size)
            for k in range(3):
                copy = pltpu.make_async_copy(held[k][i].at[span], outs[k][i].at[span], out_sems.at[p, k])
                copy.start()
                stores.append(copy)
        for copy in stores:
            copy.wait()

    return pl.pallas_call(
        kernel,
        out_shape=[shape(v.shape, F32) for v in masters] * 3 + [shape((8, 128), F32)],
        in_specs=[ANY] * (4 * n) + [VMEM],
        out_specs=[ANY] * (3 * n) + [VMEM],
        scratch_shapes=[pltpu.VMEM(v.shape, F32) for v in masters] * 4
        + [pltpu.SemaphoreType.DMA((len(pieces), 4)), pltpu.SemaphoreType.DMA((len(pieces), 3))],
        compiler_params=pltpu.CompilerParams(vmem_limit_bytes=62 * 2**20),
        name="adam_all",
    )(*masters, *drifts, *squares, *grads, sums)


def block_form(rows, columns):
    return (rows, columns) if rows % 8 == 0 else (rows * columns // 128, 128)


FIRST_AXES = ("x", "x", "y", "x")


def on_device(dims, *args):
    labels, targets, heights, loss_mask = args[:4]
    masters, drifts, squares = (args[4:12], args[12:20], args[20:28])
    class_table, code_table, attend_in, attend_mix, expand_in, shrink_out, head_weight, norm_gains = masters
    images, local_len = targets.shape
    length = local_len * 2

    layers = (attend_in, attend_mix, expand_in, shrink_out)
    *weights, start, gain, metas, allowed = gather_all(
        dims, layers, FIRST_AXES, code_table, class_table.T, norm_gains, labels, targets, heights, loss_mask, 0
    )
    qkv_w, mix_w, expand_w, shrink_w = (v.reshape(-1, v.shape[-1]) for v in weights)

    angles = rope_tables(length, HD)
    held, probs, middle = attention_forward(start, gain, angles, allowed, qkv_w, mix_w)
    grad_top, grad_head, partial, both, final = head_all(
        dims, middle, gain, metas, head_weight, expand_w, shrink_w, images, 2
    )
    grad_expand, grad_shrink, grad_qkv, grad_mix, grad_start, gain_grads, grad_head = layer_backward(
        dims, grad_top, final, middle, both, gain, expand_w, shrink_w, start, angles,
        (qkv_w, mix_w, held, probs), grad_head, 3,
    )

    grads_in = []
    for grad, shard in zip((grad_qkv, grad_mix, grad_expand, grad_shrink), layers):
        grads_in.append(grad.reshape(dims + (2,) + block_form(*shard.shape)))
    *layer_shares, code_share, class_share, gain_share, sums = scatter_all(
        dims,
        grads_in,
        FIRST_AXES,
        grad_start,
        gain_grads,
        metas,
        grad_head,
        partial,
        code_table.shape[0],
        class_table.shape[0],
        4,
    )
    layer_shares = [g.reshape(v.shape) for g, v in zip(layer_shares, layers)]
    class_share = class_share[: class_table.shape[1], : class_table.shape[0]]
    gain_share = gain_share[1:4, : norm_gains.shape[1]]
    shares = (class_share, code_share, *layer_shares, grad_head, gain_share)

    def laid(members):
        return (members[0].T, *members[1:])

    *updated, sums = adam_all(
        laid(masters), laid(drifts), laid(squares), shares, sums, RATES, DECAYS
    )
    updated = tuple(member for k in range(3) for member in laid(updated[8 * k : 8 * k + 8]))
    return updated + (sums[0, 0], sums[0, 1], sums[0, 2])


def solution(mesh):
    rows, columns = (P(("dp", "seq"), None), P(None, ("dp", "seq")))
    eight = (columns, rows, rows, rows, rows, rows, columns, columns)
    return jax.shard_map(
        functools.partial(on_device, dims_of(mesh.shape["dp"])),
        mesh=mesh,
        in_specs=(P("dp"), P("dp", "seq"), P("dp"), P("dp", "seq")) + eight * 3,
        out_specs=eight * 3 + (P(), P(), P()),
        check_vma=False,
    )
```

profile of v0, /device:TPU:0, one launch (start us, length us, event | category | flops | bytes accessed | tf_op | source)
XLA Modules:
  0.0 392.2 jit_solution(15528686503858789298)
XLA Ops:
  0.7 107.7 %gather_all.1 = (bf16[4,2,2,2,24,2304]{5,4,3,2,1,0:T(8,128)(2,1)}, bf16[4,2,2,2,24,768]{5,4,3,2,1,0:T(8,128)(2,1)}, bf16[4,2,2,2,24,4096]{5,4,3,2,1,0:T(8,128)(2...) custom-call(f32[24,2304]{1,0:T(8,128)} %refs_2_.3, ...), custom_call_target="tpu_custom_call" | custom-call | tf_op jit(solution)/shard_map/gather_all/pallas_call | solution.py:217
  108.4 10.3 %attention_forward.1 = (bf16[4,256,768]{2,1,0:T(8,128)(2,1)}, f32[12,256,256]{2,1,0:T(8,128)}, f32[256,768]{1,0:T(8,128)}) custom-call(f32[256,768]{1,0:T(8,128)} %get-tuple-element.83.start.refs_7_, f32[8,768]{1,0:T(8,128)} %get-tuple-element.84.gain.refs_1_.refs_4_, f32[2,256,128]{2,1,0:T(8,128)} %constant.2.clone.angles.refs_8_, ...), custom_call_target="tpu_custom_call" | custom-call | flops 2147483648 | bytes 16777216 | tf_op jit(solution)/shard_map/attention_forward/pallas_call | solution.py:1090
  118.7 103.8 %head_all.1 = (f32[256,768]{1,0:T(8,128)}, bf16[2,2,768,512]{3,2,1,0:T(8,128)(2,1)}, f32[8,128]{1,0:T(8,128)}, f32[256,4096]{1,0:T(8,128)}, f32[256,768]{1,0:T(8,128)}) custom-call(f32[256,768]{1,0:T(8,128)} %get-tuple-element.88.refs_0_.refs_2_, f32[8,768]{1,0:T(8,128)} %get-tuple-element.84.gain.refs_1_.refs_4_, ...), custom_call_target="tpu_custom_call" | custom-call | tf_op jit(solution)/shard_map/head_all/pallas_call | solution.py:217
  222.5 46.4 %layer_backward.1 = (bf16[768,4096]{1,0:T(8,128)(2,1)}, bf16[2048,768]{1,0:T(8,128)(2,1)}, bf16[768,2304]{1,0:T(8,128)(2,1)}, bf16[768,768]{1,0:T(8,128)(2,1)}, ...) custom-call(f32[256,768]{1,0:T(8,128)} %get-tuple-element.92.refs_0_, ...), custom_call_target="tpu_custom_call" | custom-call | tf_op jit(solution)/shard_map/layer_backward/pallas_call | solution.py:217
  268.9 106.0 %scatter_all.1 = (f32[24,2304]{1,0:T(8,128)}, f32[24,768]{1,0:T(8,128)}, f32[24,4096]{1,0:T(8,128)}, f32[64,768]{1,0:T(8,128)}, f32[512,768]{1,0:T(8,128)}, /*in...) custom-call(bf16[4,2,2,2,24,2304]{5,4,3,2,1,0:T(8,128)(2,1)} %bitcast.22, ...), custom_call_target="tpu_custom_call" | custom-call | tf_op jit(solution)/shard_map/scatter_all/pallas_call | solution.py:217
  374.9 1.5 slice.15.refs_24_
  376.5 1.3 slice.16.refs_31_
  377.7 12.9 %adam_all.1 = (f32[24,1001]{1,0:T(8,128)}, f32[512,768]{1,0:T(8,128)}, f32[24,2304]{1,0:T(8,128)}, f32[24,768]{1,0:T(8,128)}, f32[24,4096]{1,0:T(8,128)}, /*inde...) custom-call(f32[24,1001]{1,0:T(8,128)} %bitcast.30, ...), custom_call_target="tpu_custom_call" | custom-call | tf_op jit(solution)/shard_map/adam_all/pallas_call | solution.py:1325
  390.6 1.4 fusion
where the time goes:
time: 397 us; the launch traced here: 392 us
  Pallas kernels  387 us (97%)
  local copies, waits for them, and re-layouts  4.17 us (1%)
    pallas_call x4, Pallas kernels, call(): pl.pallas_call(kernel, out_shape=outs, in_specs=in_specs, out_specs=out_s...  364 us
    pallas_call x1, Pallas kernels, adam_all(): pl.pallas_call(kernel, out_shape=[shape(v.shape, F32) for v in masters] *...  12.9 us
    pallas_call x1, Pallas kernels, local_call(): pl.pallas_call(kernel, out_shape=outs, in_specs=spaces, out_specs=[VMEM]...  10.3 us

commit v1 on v0

--- a/solution.py
+++ b/solution.py
@@ -488,7 +488,8 @@
         table_out, class_out, gain_out, sums = (rest.pop(0) for _ in range(4))
         owns, halves, ones, twos, threes = ([rest.pop(0) for _ in items] for _ in range(5))
         near, far = ([rest.pop(0), rest.pop(0)] for _ in range(2))
-        lined, given, own, half, small_in, small_out, tops, mine, every, ssem, rsem, lsem = rest
+        lined, given, own, half, small_in, small_out, tops, gained_all, mine, every, *rest = rest
+        ssem, rsem, lsem = rest
         place = Place(dims)
         z, y, x, c = (place.z, place.y, place.x, place.c)
         comm = Comm(ssem, rsem, lsem)
@@ -625,7 +626,7 @@
 
         for copy in waits:
             copy.wait_recv()
-        gain_out[...] = jnp.zeros_like(gain_out)
+        gained_all[...] = jnp.zeros_like(gained_all)
         tops[...] = jnp.zeros_like(tops)
 
         @pl.loop(0, nz)
@@ -635,10 +636,10 @@
                     for core in range(2):
                         at = ((k * ny + j) * nx + i) * 2 + core
                         tops[pl.ds(at, 1), :] = small_out[k, j, i, core, 0:1, :]
-                        gain_out[...] += small_out[k, j, i, core]
-
-        value = jnp.zeros(class_out.shape, F32)
-        high = class_out.shape[1]
+                        gained_all[...] += small_out[k, j, i, core]
+
+        high = -(-classes // 128) * 128
+        value = jnp.zeros((128, high), F32)
         for r in range(label_rows):
             labels = jnp.zeros((1, 128), jnp.int32)
             for k in range(nz * plane):
@@ -653,9 +654,10 @@
                 precision=lax.Precision.HIGHEST,
                 preferred_element_type=F32,
             )
-        class_out[...] = value
-        row = lax.broadcasted_iota(jnp.int32, gain_out.shape, 0)
-        gained = jnp.where((row >= 1) & (row < 4), gain_out[...], 0.0)
+        class_out[...] = value[:columns, :classes]
+        gain_out[...] = gained_all[1:4, :columns]
+        row = lax.broadcasted_iota(jnp.int32, gained_all.shape, 0)
+        gained = jnp.where((row >= 1) & (row < 4), gained_all[...], 0.0)
         square = jnp.sum(value * value) + jnp.sum(gained * gained)
         share = head_in[...].astype(F32)
         square = square + jnp.sum(share * share)
@@ -720,6 +722,7 @@
         pltpu.VMEM(dims + (2, 8, 128), F32),
         pltpu.VMEM(dims + (2, 8, 128), F32),
         pltpu.VMEM((128 * label_rows, 128), F32),
+        pltpu.VMEM((8, 128), F32),
         pltpu.VMEM(partial.shape, F32),
         pltpu.VMEM(dims + (2,) + partial.shape, F32),
         sems(total),
@@ -727,8 +730,8 @@
         sems(len(items)),
     ]
     outs = [shape(t, F32) for t in shapes]
-    high = -(-classes // 128) * 128
-    outs += [shape(block, F32), shape((128, high), F32), shape((8, 128), F32), shape(partial.shape, F32)]
+    outs += [shape(block, F32), shape((columns, classes), F32), shape((3, columns), F32)]
+    outs += [shape(partial.shape, F32)]
     return call(
         kernel, outs, [ANY] * n + [VMEM] * 5, [VMEM] * (n + 4), scratch,
         cid, "scatter_all", (*grads, rows, gains, metas, head, partial), 60 * 2**20,
@@ -794,11 +797,11 @@
                 tall = jnp.broadcast_to(codes, (128, 128)).T.astype(jnp.int32)
                 marks_in[s, 128 * part : 128 * part + 128] = tall[:, :lanes] - z * (blocks * columns)
         gather.forward()
-        gather.settle()
         for s in turns[:2]:
             comm.gone(arriving[s])
         for s in turns[2:]:
             arriving[s] = comm.send(lined.at[0], lined.at[s], place.dev(z=s))
+        gather.settle()
         gather.arrive()
 
         def block(k):
@@ -821,30 +824,32 @@
             totals[...] = jnp.zeros_like(totals)
             picks[...] = jnp.zeros_like(picks)
 
-            @pl.loop(0, blocks)
-            def _(k):
-                logits = logits_of(s, k)
-                if keep:
-                    exps[k, at] = logits
+            @pl.loop(0, blocks // 2)
+            def _(pair):
                 high, found = (peaks[...], picks[...])
-                for piece, hit in zip(split(logits), hits(s, k)):
-                    high = jnp.maximum(high, piece)
-                    found = found + jnp.where(hit, piece, 0.0)
+                for k in (2 * pair, 2 * pair + 1):
+                    logits = logits_of(s, k)
+                    if keep:
+                        exps[k, at] = logits
+                    for piece, hit in zip(split(logits), hits(s, k)):
+                        high = jnp.maximum(high, piece)
+                        found = found + jnp.where(hit, piece, 0.0)
                 peaks[...] = high
                 picks[...] = found
 
             peak = jnp.max(peaks[...], axis=1, keepdims=True)
             peaks[...] = jnp.broadcast_to(peak, (length, lanes))
 
-            @pl.loop(0, blocks)
-            def _(k):
-                logits = exps[k, at] if keep else logits_of(s, k)
+            @pl.loop(0, blocks // 2)
+            def _(pair):
                 total = totals[...]
-                for q, piece in enumerate(split(logits)):
-                    power = jnp.exp(piece - peaks[...])
-                    if keep:
-                        exps[k, at, lanes * q : lanes * (q + 1)] = power
-                    total = total + power
+                for k in (2 * pair, 2 * pair + 1):
+                    logits = exps[k, at] if keep else logits_of(s, k)
+                    for q, piece in enumerate(split(logits)):
+                        power = jnp.exp(piece - peaks[...])
+                        if keep:
+                            exps[k, at, lanes * q : lanes * (q + 1)] = power
+                        total = total + power
                 totals[...] = total
 
             if not keep:
@@ -894,21 +899,22 @@
             columned[1] = jnp.broadcast_to(tall[:, 1:2], (length, lanes))
             partial[...] = jnp.zeros_like(partial)
 
-            @pl.loop(0, blocks)
-            def _(k):
-                if keep:
-                    powers = split(exps[k, at])
-                else:
-                    powers = [jnp.exp(piece - exps[s]) for piece in split(logits_of(s, k))]
-                pieces = []
-                for power, hit in zip(powers, hits(s, k)):
-                    grad = power * columned[0] - jnp.where(hit, columned[1], 0.0)
-                    pieces.append(grad.astype(BF))
-                grad = jnp.concatenate(pieces, axis=1) if groups > 1 else pieces[0]
-                grads[k, at] = grad
-                partial[...] += lax.dot_general(
-                    grad, block(k), (((1,), (1,)), ((), ())), preferred_element_type=F32
-                )
+            @pl.loop(0, blocks // 2)
+            def _(pair):
+                added = partial[...]
+                for k in (2 * pair, 2 * pair + 1):
+                    if keep:
+                        powers = split(exps[k, at])
+                    else:
+                        powers = [jnp.exp(piece - exps[s]) for piece in split(logits_of(s, k))]
+                    parts = []
+                    for power, hit in zip(powers, hits(s, k)):
+                        grad = power * columned[0] - jnp.where(hit, columned[1], 0.0)
+                        parts.append(grad.astype(BF))
+                    grad = jnp.concatenate(parts, axis=1) if groups > 1 else parts[0]
+                    grads[k, at] = grad
+                    added = added + times_turned(grad, block(k))
+                partial[...] = added
 
         coming_in = []
         for s in range(1, nz):
@@ -1271,8 +1277,8 @@
         ins = [refs[n * k : n * (k + 1)] for k in range(4)]
         sums_in = refs[4 * n]
         outs = [refs[4 * n + 1 + n * k : 4 * n + 1 + n * (k + 1)] for k in range(3)]
-        sums_out = refs[7 * n + 1]
-        rest = refs[7 * n + 2 :]
+        sums_out = refs[7 * n + 1 : 7 * n + 4]
+        rest = refs[7 * n + 4 :]
         held = [rest[n * k : n * (k + 1)] for k in range(4)]
         in_sems, out_sems = rest[4 * n :]
         loads, stores = ([], [])
@@ -1284,13 +1290,15 @@
                     for k in range(4)
                 ]
             )
-            for copy in loads[-1]:
+        ahead = 3
+        for p in range(ahead):
+            for copy in loads[p]:
                 copy.start()
         row = sums_in[0:1]
         norm = jnp.sqrt(row[:, 0:1]) / row[:, 2:3]
         factor = CLIP_NORM / jnp.maximum(norm, CLIP_NORM) / row[:, 2:3]
-        lane = lax.broadcasted_iota(jnp.int32, (8, 128), 1)
-        sums_out[...] = jnp.where(lane == 0, norm, sums_in[...])
+        for out, value in zip(sums_out, (norm, row[:, 1:2], row[:, 2:3])):
+            out[...] = value
 
         def update(i, span):
             fresh, moment, second = adam_update(
@@ -1306,6 +1314,9 @@
         for p, (i, at, size) in enumerate(pieces):
             for copy in loads[p]:
                 copy.wait()
+            if p + ahead < len(pieces):
+                for copy in loads[p + ahead]:
+                    copy.start()
             if size % 8:
                 update(i, slice(at, at + size))
             else:
@@ -1324,9 +1335,9 @@
 
     return pl.pallas_call(
         kernel,
-        out_shape=[shape(v.shape, F32) for v in masters] * 3 + [shape((8, 128), F32)],
+        out_shape=[shape(v.shape, F32) for v in masters] * 3 + [shape((1, 1), F32)] * 3,
         in_specs=[ANY] * (4 * n) + [VMEM],
-        out_specs=[ANY] * (3 * n) + [VMEM],
+        out_specs=[ANY] * (3 * n) + [VMEM] * 3,
         scratch_shapes=[pltpu.VMEM(v.shape, F32) for v in masters] * 4
         + [pltpu.SemaphoreType.DMA((len(pieces), 4)), pltpu.SemaphoreType.DMA((len(pieces), 3))],
         compiler_params=pltpu.CompilerParams(vmem_limit_bytes=62 * 2**20),
@@ -1381,18 +1392,15 @@
         4,
     )
     layer_shares = [g.reshape(v.shape) for g, v in zip(layer_shares, layers)]
-    class_share = class_share[: class_table.shape[1], : class_table.shape[0]]
-    gain_share = gain_share[1:4, : norm_gains.shape[1]]
     shares = (class_share, code_share, *layer_shares, grad_head, gain_share)
 
     def laid(members):
         return (members[0].T, *members[1:])
 
-    *updated, sums = adam_all(
-        laid(masters), laid(drifts), laid(squares), shares, sums, RATES, DECAYS
-    )
+    updated = adam_all(laid(masters), laid(drifts), laid(squares), shares, sums, RATES, DECAYS)
+    sums = updated[24:]
     updated = tuple(member for k in range(3) for member in laid(updated[8 * k : 8 * k + 8]))
-    return updated + (sums[0, 0], sums[0, 1], sums[0, 2])
+    return updated + tuple(member.reshape(()) for member in sums)
 
 
 def solution(mesh):

time: 397 us -> 388 us (0.977)
  local copies, waits for them, and re-layouts: 4.17 us -> 0 us
  Pallas kernels: 387 us -> 383 us
    pallas_call x4, Pallas kernels: 364 us -> 359 us  [call(): pl.pallas_call(kernel, out_shape=outs, in_specs=in_specs, out_specs=out_s...]
    slice x3 -> x0, local copies, waits for them, and re-layouts: 4.17 us -> none  [the longest x1 1.53 us: on_device(): class_share = class_share[:class_table.shape[1], :class_table.shape[0]]]
where the time goes in v1:
time: 388 us; the launch traced here: 384 us
  Pallas kernels  383 us (99%)
    pallas_call x4, Pallas kernels, call(): pl.pallas_call(kernel, out_shape=outs, in_specs=in_specs, out_specs=out_s...  359 us
    pallas_call x1, Pallas kernels, adam_all(): pl.pallas_call(kernel, out_shape=[shape(v.shape, F32) for v in masters] *...  13.5 us
    pallas_call x1, Pallas kernels, local_call(): pl.pallas_call(kernel, out_shape=outs, in_specs=spaces, out_specs=[VMEM]...  10.3 us

profile of v1, /device:TPU:0, one launch (start us, length us, event | category | flops | bytes accessed | tf_op | source)
XLA Modules:
  0.0 383.8 jit_solution(2264881491058939623)
XLA Ops:
  0.7 107.7 %gather_all.1 = (bf16[4,2,2,2,24,2304]{5,4,3,2,1,0:T(8,128)(2,1)}, bf16[4,2,2,2,24,768]{5,4,3,2,1,0:T(8,128)(2,1)}, bf16[4,2,2,2,24,4096]{5,4,3,2,1,0:T(8,128)(2...) custom-call(f32[24,2304]{1,0:T(8,128)} %refs_2_.3, ...), custom_call_target="tpu_custom_call" | custom-call | tf_op jit(solution)/shard_map/gather_all/pallas_call | solution.py:217
  108.3 10.3 %attention_forward.1 = (bf16[4,256,768]{2,1,0:T(8,128)(2,1)}, f32[12,256,256]{2,1,0:T(8,128)}, f32[256,768]{1,0:T(8,128)}) custom-call(f32[256,768]{1,0:T(8,128)} %get-tuple-element.85.start.refs_7_, f32[8,768]{1,0:T(8,128)} %get-tuple-element.86.gain.refs_1_.refs_4_, f32[2,256,128]{2,1,0:T(8,128)} %constant.2.clone.angles.refs_8_, ...), custom_call_target="tpu_custom_call" | custom-call | flops 2147483648 | bytes 16777216 | tf_op jit(solution)/shard_map/attention_forward/pallas_call | solution.py:1096
  118.6 98.1 %head_all.1 = (f32[256,768]{1,0:T(8,128)}, bf16[2,2,768,512]{3,2,1,0:T(8,128)(2,1)}, f32[8,128]{1,0:T(8,128)}, f32[256,4096]{1,0:T(8,128)}, f32[256,768]{1,0:T(8,128)}) custom-call(f32[256,768]{1,0:T(8,128)} %get-tuple-element.90.refs_0_.refs_2_, f32[8,768]{1,0:T(8,128)} %get-tuple-element.86.gain.refs_1_.refs_4_, ...), custom_call_target="tpu_custom_call" | custom-call | tf_op jit(solution)/shard_map/head_all/pallas_call | solution.py:217
  216.7 49.0 %layer_backward.1 = (bf16[768,4096]{1,0:T(8,128)(2,1)}, bf16[2048,768]{1,0:T(8,128)(2,1)}, bf16[768,2304]{1,0:T(8,128)(2,1)}, bf16[768,768]{1,0:T(8,128)(2,1)}, ...) custom-call(f32[256,768]{1,0:T(8,128)} %get-tuple-element.94.refs_0_, ...), custom_call_target="tpu_custom_call" | custom-call | tf_op jit(solution)/shard_map/layer_backward/pallas_call | solution.py:217
  265.7 104.4 %scatter_all.1 = (f32[24,2304]{1,0:T(8,128)}, f32[24,768]{1,0:T(8,128)}, f32[24,4096]{1,0:T(8,128)}, f32[64,768]{1,0:T(8,128)}, f32[512,768]{1,0:T(8,128)}, /*in...) custom-call(bf16[4,2,2,2,24,2304]{5,4,3,2,1,0:T(8,128)(2,1)} %bitcast.22, ...), custom_call_target="tpu_custom_call" | custom-call | tf_op jit(solution)/shard_map/scatter_all/pallas_call | solution.py:217
  370.1 13.5 %adam_all.1 = (f32[24,1001]{1,0:T(8,128)}, f32[512,768]{1,0:T(8,128)}, f32[24,2304]{1,0:T(8,128)}, f32[24,768]{1,0:T(8,128)}, f32[24,4096]{1,0:T(8,128)}, /*inde...) custom-call(f32[24,1001]{1,0:T(8,128)} %bitcast.30, ...), custom_call_target="tpu_custom_call" | custom-call | tf_op jit(solution)/shard_map/adam_all/pallas_call | solution.py:1336

commit v2 on v1

--- a/solution.py
+++ b/solution.py
@@ -496,15 +496,7 @@
         kept = []
         for i, (a, span, cols, _) in enumerate(items):
             kept.append(comm.keep(parts[a].at[:, :, :, c, span, cols], owns[i]))
-        lane = lax.broadcasted_iota(jnp.int32, (8, 128), 1)
-        top = jnp.concatenate([rows_in[0:1], gains_in[0:3], jnp.zeros((4, width), F32)], axis=0)
-        for d in range(2 * nz * plane):
-            k, core = divmod(d, 2)
-            piece = pltpu.roll(top, (width - columns * d) % width, 1)[:, :128]
-            small_in[k // plane, k // nx % ny, k % nx, core] = jnp.where(lane < columns, piece, 0.0)
         greet(place, all_offsets(dims))
-        waits = small_exchange(comm, place, lambda *spot: small_in.at[spot], small_out, False)
-        small_out[z, y, x, c] = small_in[z, y, x, c]
         pair, got_one, got_two, third = ({}, {}, {}, {})
 
         def set_out(g):
@@ -588,6 +580,14 @@
 
         set_out(0)
         set_out(1)
+        lane = lax.broadcasted_iota(jnp.int32, (8, 128), 1)
+        top = jnp.concatenate([rows_in[0:1], gains_in[0:3], jnp.zeros((4, width), F32)], axis=0)
+        for d in range(2 * nz * plane):
+            k, core = divmod(d, 2)
+            piece = pltpu.roll(top, (width - columns * d) % width, 1)[:, :128]
+            small_in[k // plane, k // nx % ny, k % nx, core] = jnp.where(lane < columns, piece, 0.0)
+        waits = small_exchange(comm, place, lambda *spot: small_in.at[spot], small_out, False)
+        small_out[z, y, x, c] = small_in[z, y, x, c]
         lined[0] = rows_in[...].astype(BF)
         lines = [comm.send(lined.at[0], lined.at[s], place.dev(z=s)) for s in range(1, nz)]
         count = len(order)
@@ -1317,13 +1317,14 @@
             if p + ahead < len(pieces):
                 for copy in loads[p + ahead]:
                     copy.start()
-            if size % 8:
+            strip = 32 if size % 32 == 0 else 8
+            if size % strip:
                 update(i, slice(at, at + size))
             else:
 
-                @pl.loop(0, size // 8)
-                def _(k, i=i, at=at):
-                    update(i, pl.ds(pl.multiple_of(at + 8 * k, 8), 8))
+                @pl.loop(0, size // strip)
+                def _(k, i=i, at=at, strip=strip):
+                    update(i, pl.ds(pl.multiple_of(at + strip * k, strip), strip))
 
             span = pl.ds(at, size)
             for k in range(3):

time: 388 us -> 388 us (level)
  no operation moved by 1% of the time
where the time goes in v2:
time: 388 us; the launch traced here: 383 us
  Pallas kernels  382 us (98%)
    pallas_call x4, Pallas kernels, call(): pl.pallas_call(kernel, out_shape=outs, in_specs=in_specs, out_specs=out_s...  359 us
    pallas_call x1, Pallas kernels, adam_all(): pl.pallas_call(kernel, out_shape=[shape(v.shape, F32) for v in masters] *...  12.8 us
    pallas_call x1, Pallas kernels, local_call(): pl.pallas_call(kernel, out_shape=outs, in_specs=spaces, out_specs=[VMEM]...  10.3 us

profile of v2, /device:TPU:0, one launch (start us, length us, event | category | flops | bytes accessed | tf_op | source)
XLA Modules:
  0.0 383.4 jit_solution(2549058695540992582)
XLA Ops:
  0.7 107.7 %gather_all.1 = (bf16[4,2,2,2,24,2304]{5,4,3,2,1,0:T(8,128)(2,1)}, bf16[4,2,2,2,24,768]{5,4,3,2,1,0:T(8,128)(2,1)}, bf16[4,2,2,2,24,4096]{5,4,3,2,1,0:T(8,128)(2...) custom-call(f32[24,2304]{1,0:T(8,128)} %refs_2_.3, ...), custom_call_target="tpu_custom_call" | custom-call | tf_op jit(solution)/shard_map/gather_all/pallas_call | solution.py:217
  108.3 10.3 %attention_forward.1 = (bf16[4,256,768]{2,1,0:T(8,128)(2,1)}, f32[12,256,256]{2,1,0:T(8,128)}, f32[256,768]{1,0:T(8,128)}) custom-call(f32[256,768]{1,0:T(8,128)} %get-tuple-element.85.start.refs_7_, f32[8,768]{1,0:T(8,128)} %get-tuple-element.86.gain.refs_1_.refs_4_, f32[2,256,128]{2,1,0:T(8,128)} %constant.2.clone.angles.refs_8_, ...), custom_call_target="tpu_custom_call" | custom-call | flops 2147483648 | bytes 16777216 | tf_op jit(solution)/shard_map/attention_forward/pallas_call | solution.py:1096
  118.6 98.1 %head_all.1 = (f32[256,768]{1,0:T(8,128)}, bf16[2,2,768,512]{3,2,1,0:T(8,128)(2,1)}, f32[8,128]{1,0:T(8,128)}, f32[256,4096]{1,0:T(8,128)}, f32[256,768]{1,0:T(8,128)}) custom-call(f32[256,768]{1,0:T(8,128)} %get-tuple-element.90.refs_0_.refs_2_, f32[8,768]{1,0:T(8,128)} %get-tuple-element.86.gain.refs_1_.refs_4_, ...), custom_call_target="tpu_custom_call" | custom-call | tf_op jit(solution)/shard_map/head_all/pallas_call | solution.py:217
  216.7 49.3 %layer_backward.1 = (bf16[768,4096]{1,0:T(8,128)(2,1)}, bf16[2048,768]{1,0:T(8,128)(2,1)}, bf16[768,2304]{1,0:T(8,128)(2,1)}, bf16[768,768]{1,0:T(8,128)(2,1)}, ...) custom-call(f32[256,768]{1,0:T(8,128)} %get-tuple-element.94.refs_0_, ...), custom_call_target="tpu_custom_call" | custom-call | tf_op jit(solution)/shard_map/layer_backward/pallas_call | solution.py:217
  266.0 104.3 %scatter_all.1 = (f32[24,2304]{1,0:T(8,128)}, f32[24,768]{1,0:T(8,128)}, f32[24,4096]{1,0:T(8,128)}, f32[64,768]{1,0:T(8,128)}, f32[512,768]{1,0:T(8,128)}, /*in...) custom-call(bf16[4,2,2,2,24,2304]{5,4,3,2,1,0:T(8,128)(2,1)} %bitcast.22, ...), custom_call_target="tpu_custom_call" | custom-call | tf_op jit(solution)/shard_map/scatter_all/pallas_call | solution.py:217
  370.4 12.8 %adam_all.1 = (f32[24,1001]{1,0:T(8,128)}, f32[512,768]{1,0:T(8,128)}, f32[24,2304]{1,0:T(8,128)}, f32[24,768]{1,0:T(8,128)}, f32[24,4096]{1,0:T(8,128)}, /*inde...) custom-call(f32[24,1001]{1,0:T(8,128)} %bitcast.30, ...), custom_call_target="tpu_custom_call" | custom-call | tf_op jit(solution)/shard_map/adam_all/pallas_call | solution.py:1337
